TPU v7x, 256 devices: a whole 4x4x8 slice. The times are simulated.
256 devices in a mesh: lat: 8 (over x, y_hi), lon: 8 (over z), tp: 4 (over y_lo, core).
Axes of the slice: x: 4, y: 4 (y_hi: 2, y_lo: 2; y = y_hi * 2 + y_lo), z: 8, core: 2. Of those that a mesh axis runs over, the one named last changes fastest.
Arguments:
- tokens: bfloat16 [2, 192, 384, 512], P(None, 'lat', 'lon'), may hold values from -6 to 6
- cotangent: bfloat16 [2, 192, 384, 512], P(None, 'lat', 'lon'), may hold values from -6 to 6
- norm_gain: float32 [512], replicated, may hold values from 0.1 to 1.9
- norm_bias: float32 [512], replicated, may hold values from -3 to 3
- w_qkv: bfloat16 [512, 3, 512], P(None, None, 'tp'), as said below
- w_out: bfloat16 [512, 512], P('tp'), may hold values from -0.25 to 0.25
Outputs:
- grad_tokens: bfloat16 [2, 192, 384, 512], P(None, 'lat', 'lon')
- grad_gain: float32 [512], replicated
- grad_bias: float32 [512], replicated
- grad_qkv: float32 [512, 3, 512], P(None, None, 'tp')
- grad_out: float32 [512, 512], P('tp')
Inputs may be any that keep to these rules, and one draw needn't show every extreme that they name: `w_qkv`: a projection matrix of the normalised tokens to queries, keys and values.
All inputs are finite; a program needn't handle non-finite values.
Results may differ from a plain program's by a relative error of at most 0.02.
Values may be sent and summed in bfloat16 or wider, within the bound.
No kernel may reach another device: no remote copies, remote signals or barrier semaphores. Data moves between devices by JAX's collectives and lax.ppermute only.
A program may use at most 128 MiB of HBM per device.

v0:
```python
import jax
import jax.numpy as jnp
from jax import lax
from jax.experimental import pallas as pl
from jax.experimental.pallas import tpu as pltpu
from jax.sharding import PartitionSpec as P

HEAD = 64
SLAT = 3
SLON = 6
SPAN = 144
D = 512
BF = jnp.bfloat16
F32 = jnp.float32
NT = (((1,), (1,)), ((), ()))
NN = (((1,), (0,)), ((), ()))
TN = (((0,), (0,)), ((), ()))
FLOPS = 4_000_000_000, 50_000_000, 50_000_000, 50_000_000, 8_000_000_000
INSIDE = pl.BlockSpec(memory_space=pltpu.VMEM)
ANYWHERE = pl.BlockSpec(memory_space=pl.ANY)
VMEM_BYTES = 32 * 1024 * 1024

PLACE = (
    ((0, 0), (2, 0), (0, 1), (2, 1)),
    ((1, 0), (0, 2), (1, 1), (1, 2)),
    ((3, 0), (3, 2), (3, 1), (2, 2)),
    ((0, 3), (1, 3), (2, 3), (3, 3)),
)


def dot(a, b, form):
    return lax.dot_general(a, b, form, preferred_element_type=F32)


def move(block, axes, step):
    sizes = [lax.axis_size(axis) for axis in axes]
    total = 1
    for size in sizes:
        total *= size

    def index(coords):
        flat = 0
        for size, coord in zip(sizes, coords):
            flat = flat * size + coord % size
        return flat

    def coords(flat):
        out = []
        for size in reversed(sizes):
            out.append(flat % size)
            flat //= size
        return tuple(reversed(out))

    return lax.ppermute(block, axes, [(i, index(step(*coords(i)))) for i in range(total)])


def even_window(ref, row, column):
    rows = slice(row, row + 6)
    top = lax.broadcasted_iota(jnp.int32, (6, 8, D), 1) < 4
    full = ref[:, rows, column : column + 8, :].reshape(96, D)
    rest = jnp.where(
        top, ref[0, rows, column + 8 : column + 16, :], ref[1, rows, column + 4 : column + 12, :]
    )
    return jnp.concatenate([full, rest.reshape(48, D)], 0)


def odd_window(ref, row, column):
    rows = slice(row, row + 6)
    top = lax.broadcasted_iota(jnp.int32, (6, 8, D), 1) < 4
    full = ref[:, rows, column + 4 : column + 12, :].reshape(96, D)
    rest = jnp.where(
        top, ref[0, rows, column : column + 8, :], ref[1, rows, column - 4 : column + 4, :]
    )
    return jnp.concatenate([full, rest.reshape(48, D)], 0)


def normalised(x):
    mean = jnp.sum(x, axis=-1, keepdims=True) * (1.0 / D)
    centered = x - mean
    inv_std = lax.rsqrt(jnp.sum(centered * centered, axis=-1, keepdims=True) * (1.0 / D) + 1e-05)
    return centered * inv_std, inv_std


def window_steps(xs, gs, gain, bias, weights, masks, sums, gb_acc):
    left = lax.broadcasted_iota(jnp.int32, (SPAN, 128), 1) < HEAD
    zero = jnp.zeros((SPAN, 128), BF)

    def by_head(a):
        parts = [(jnp.where(left, half, zero), jnp.where(left, zero, half)) for half in (a[:, :128], a[:, 128:])]
        rows = [jnp.concatenate([part, zero], 1) for part in parts[0]]
        return jnp.concatenate(rows + [jnp.concatenate([zero, part], 1) for part in parts[1]], 0)

    count = range(len(xs))
    unit = [normalised(x.astype(F32))[0] for x in xs]
    normed = [(u * gain + bias).astype(BF) for u in unit]
    both = [(n, w) for n in count for w in range(2)]
    to_heads = jnp.concatenate([weights[w][0:384, :] for w in range(2)], 0)
    to_keys = jnp.concatenate([weights[w][r : r + 128, :] for r in (128, 256) for w in range(2)], 0)
    to_grads = jnp.concatenate([weights[w][384:512, :] for w in range(2)], 0)
    all_proj = [dot(to_heads, normed[n], NT).astype(BF) for n in count]
    all_kv = [dot(normed[n], to_keys, NT).astype(BF) for n in count]
    all_da = [dot(to_grads, gs[n], NT).astype(BF) for n in count]
    proj = {(n, w): all_proj[n][384 * w : 384 * w + 384] for n, w in both}
    da = {(n, w): all_da[n][128 * w : 128 * w + 128] for n, w in both}
    q = {i: p[0:128] * 0.125 for i, p in proj.items()}
    k = {i: p[128:256] for i, p in proj.items()}
    v = {i: p[256:384] for i, p in proj.items()}
    all_q = [jnp.concatenate([q[n, 0], q[n, 1]], 0) for n in count]
    scores = [dot(by_head(all_kv[n][:, :256]), all_q[n], NN) for n in count]
    d_probs = [dot(by_head(all_kv[n][:, 256:]), all_da[n], NN) for n in count]
    heads = [(i, head) for i in both for head in range(2)]
    probs, ds = {}, {}
    for i, head in heads:
        at = (2 * i[1] + head) * SPAN
        s = scores[i[0]][at : at + SPAN]
        if masks is not None:
            s = s + masks[i[0]]
        raised = jnp.exp(s - jnp.max(s, axis=0, keepdims=True))
        probs[i, head] = (raised * (1.0 / jnp.sum(raised, axis=0, keepdims=True))).astype(BF)
    for i, head in heads:
        pf = probs[i, head].astype(F32)
        at = (2 * i[1] + head) * SPAN
        dp = d_probs[i[0]][at : at + SPAN]
        ds[i, head] = (pf * (dp - jnp.sum(pf * dp, axis=0, keepdims=True))).astype(BF)
    cuts = [slice(0, HEAD), slice(HEAD, 2 * HEAD)]
    att = {(i, h): dot(v[i][cuts[h]], probs[i, h], NN).astype(BF) for i, h in heads}
    dv = {(i, h): dot(da[i][cuts[h]], probs[i, h], NT).astype(BF) for i, h in heads}
    dq = {(i, h): (dot(k[i][cuts[h]], ds[i, h], NN) * 0.125).astype(BF) for i, h in heads}
    dk = {(i, h): dot(q[i][cuts[h]], ds[i, h], NT).astype(BF) for i, h in heads}
    attended = {i: jnp.concatenate([att[i, 0], att[i, 1]], 0) for i in both}
    d_project = {
        i: jnp.concatenate([dq[i, 0], dq[i, 1], dk[i, 0], dk[i, 1], dv[i, 0], dv[i, 1]], 0) for i in both
    }
    d_heads = [jnp.concatenate([d_project[n, w] for w in range(2)], 0) for n in count]
    heads_out = [jnp.concatenate([attended[n, w] for w in range(2)], 0) for n in count]
    d_weights = sum(dot(d_heads[n], normed[n], NN) for n in count)
    d_out = sum(dot(heads_out[n], gs[n], NN) for n in count)
    for w in range(2):
        sums[w][0:384, :] += d_weights[384 * w : 384 * w + 384]
        sums[w][384:512, :] += d_out[128 * w : 128 * w + 128]
    dn = [dot(d_heads[n], to_heads, TN) for n in count]
    gb_acc[0:8, :] += sum(jnp.sum((dn[n] * unit[n]).reshape(SPAN // 8, 8, D), axis=0) for n in count)
    gb_acc[8:16, :] += sum(jnp.sum(dn[n].reshape(SPAN // 8, 8, D), axis=0) for n in count)
    return [d.astype(BF) for d in dn]


def group_steps(scalars, windows, masks, gain_ref, bias_ref, weights, sums, gb_acc, out):
    xs, gs = ([ref[n] for n in range(2)] for ref in windows)
    added = None if masks is None else [masks[scalars[n]] for n in range(2)]
    dn = window_steps(xs, gs, gain_ref[...], bias_ref[...], weights, added, sums, gb_acc)
    for n in range(2):
        out[0, n] = dn[n]


def inner_kernel(group):
    def kernel(scalars, *refs):
        core = scalars[2]
        if group == 0:
            hbm, rows_in, refs = refs[:2], refs[2:4], refs[4:]
            gain, bias, mine, theirs, dn, sum_mine, sum_theirs, gb, *tiles = refs[:10]
            stage, xw, gw, load_sems = refs[10:]
            pieces = ((3 + 12 * core, 6), (9, 6), (15 - 12 * core, 6), (21, 3))
            loads = [
                [
                    pltpu.make_async_copy(
                        hbm[n].at[:, pl.ds(start, rows)], tiles[n].at[:, pl.ds(start, rows)], load_sems.at[n, m]
                    )
                    for n in range(2)
                ]
                for m, (start, rows) in enumerate(pieces)
            ]
            for piece in loads:
                for load in piece:
                    load.start()
            sum_mine[...] = jnp.zeros_like(sum_mine)
            sum_theirs[...] = jnp.zeros_like(sum_theirs)
            gb[...] = jnp.zeros_like(gb)
            rows = []
        else:
            tiles, refs = refs[:2], refs[2:]
            gain, bias, mine, theirs = refs[:4]
            dn, sum_mine, sum_theirs, gb, stage, xw, gw = refs[7:]
            loads = []
            rows = [1 - core, 1]
        for tile, out in zip(rows_in if group == 0 else tiles, (xw, gw)):
            if group == 0:
                stage[...] = tile[...].astype(F32)
            for n, row in enumerate(rows):
                stage[:, 6 * n : 6 * n + 6, :, :] = tile[:, pl.ds(3 + 6 * row, 6), :, :].astype(F32)
            for c in range(2):

                @pl.when(core == c)
                def _():
                    for n in range(2):
                        column = PLACE[group][2 * n + c][1]
                        out[n] = even_window(stage, 6 * n * group, SLON + 12 * column).astype(BF)

        group_steps(scalars, (xw, gw), None, gain, bias, (mine, theirs), (sum_mine, sum_theirs), gb, dn)
        for piece in loads:
            for load in piece:
                load.wait()

    return kernel


def row_kernel(
    scalars, tok, cot, h_lat, gain_ref, bias_ref, mine, theirs, in_mine, in_theirs, gb_in,
    dn, sum_mine, sum_theirs, gb, stage, xw, gw, masks,
):
    fill_masks(masks)
    core = scalars[2]
    for part, tile, out in ((0, tok, xw), (2, cot, gw)):
        stage[:, 0:9, :, :] = tile[:, 15:24, :, :].astype(F32)
        for c in range(2):

            @pl.when(core == c)
            def _():
                stage[:, 9:12, 16 * c : 16 * c + 32, :] = h_lat[part : part + 2].astype(F32)
                for n in range(2):
                    row, column = PLACE[2][2 * n + c]
                    out[n] = even_window(stage, 6 * (row - 2), SLON + 12 * column).astype(BF)

    group_steps(scalars, (xw, gw), masks, gain_ref, bias_ref, (mine, theirs), (sum_mine, sum_theirs), gb, dn)


def column_kernel(
    scalars, tok, cot, h_lat, h_lon, h_cor, gain_ref, bias_ref, mine, theirs, in_mine, in_theirs, gb_in,
    dn, sum_mine, sum_theirs, gb, payload_mine, first_theirs, second_theirs, small,
    stage, xw, gw, masks,
):
    fill_masks(masks)
    core = scalars[2]
    for part, tile, out in ((0, tok, xw), (2, cot, gw)):
        for n in range(2):
            rows = pl.ds(3 + 12 * n + 6 * core, 3)
            stage[:, 6 * n : 6 * n + 3, 0:16, :] = tile[:, rows, 32:48, :].astype(F32)
            stage[:, 6 * n : 6 * n + 6, 16:24, :] = h_lon[part : part + 2, 6 * n : 6 * n + 6].astype(F32)
        stage[:, 3:6, 0:16, :] = tile[:, pl.ds(6 + 6 * core, 3), 32:48, :].astype(F32)

        @pl.when(core == 0)
        def _():
            stage[:, 9:12, 0:16, :] = tile[:, 18:21, 32:48, :].astype(F32)

        @pl.when(core == 1)
        def _():
            stage[:, 9:12, 0:16, :] = h_lat[part : part + 2, :, 16:32, :].astype(F32)
            stage[:, 9:12, 16:24, :] = h_cor[part : part + 2].astype(F32)

        for n in range(2):
            out[n] = odd_window(stage, 6 * n, 10).astype(BF)
    group_steps(scalars, (xw, gw), masks, gain_ref, bias_ref, (mine, theirs), (sum_mine, sum_theirs), gb, dn)
    for t in range(4):
        for sums, payload in (sum_mine, (payload_mine, t)), (sum_theirs, ((first_theirs, second_theirs)[t // 2], t % 2)):
            ref, place = payload
            if t < 3:
                rows = sums[128 * t : 128 * t + 128, :].T
            else:
                rows = jnp.concatenate([sums[384:512, 128 * n : 128 * n + 128] for n in range(4)], 0)
            ref[512 * place : 512 * place + 512, :] = rows.astype(ref.dtype)
    pair = [jnp.sum(gb[8 * n : 8 * n + 8, :], axis=0, keepdims=True) for n in range(2)]
    small[...] = jnp.concatenate([s[:, 128 * n : 128 * n + 128] for s in pair for n in range(4)], 0)


def fill_masks(masks):
    key_row = lax.broadcasted_iota(jnp.int32, (SPAN, SPAN), 0) // 8 % 6
    query_row = lax.broadcasted_iota(jnp.int32, (SPAN, SPAN), 1) // 8 % 6
    masks[0] = jnp.zeros((SPAN, SPAN), F32)
    masks[1] = jnp.where((key_row >= 3) != (query_row >= 3), -1e30, 0.0)


def whole(shape):
    return pl.BlockSpec(shape, lambda i, scalars: (0,) * len(shape))


SUMS = [((512, D), F32), ((512, D), F32), ((16, D), F32)]


def kernel_call(kernel, steps, scalars, blocks, args, outs, scratch=(), waits=(), aliases=None, flops=5_000_000):
    many = isinstance(outs, list)
    out_list = outs if many else [outs]
    first = 1 + len(blocks) + len(args)

    def body(*refs):
        kernel(*refs[:first], *refs[first + len(waits) :])

    result = pl.pallas_call(
        body,
        grid_spec=pltpu.PrefetchScalarGridSpec(
            num_scalar_prefetch=1,
            grid=(steps,),
            in_specs=[spec for _, spec in blocks] + [INSIDE] * len(args) + [ANYWHERE] * len(waits),
            out_specs=[out[2] if len(out) > 2 else INSIDE for out in out_list],
            scratch_shapes=scratch,
        ),
        out_shape=[
            pltpu.HBM(*out[:2]) if len(out) > 2 else jax.ShapeDtypeStruct(*out) for out in out_list
        ],
        input_output_aliases=aliases or {},
        compiler_params=pltpu.CompilerParams(
            dimension_semantics=("arbitrary",), vmem_limit_bytes=VMEM_BYTES
        ),
        cost_estimate=pl.CostEstimate(flops=flops, bytes_accessed=1_000_000, transcendentals=0),
    )(
        scalars,
        *(pltpu.with_memory_space_constraint(array, pltpu.HBM) for array, _ in blocks),
        *args,
        *waits,
    )
    return result if many else result[0]


def group_call(kernel, scalars, arrays, args, sums, extra_out, rows, scratch, flops, waits=()):
    shape = (1, 2, SPAN, D)
    outs = [(shape, BF, whole(shape))] + SUMS + extra_out
    start = 1 + len(arrays) + len(args)
    aliases = {start + n: 1 + n for n in range(len(sums))}
    stage = [pltpu.VMEM(rows + (D,), F32)] + [pltpu.VMEM((2, SPAN, D), BF)] * 2
    blocks = [(a, ANYWHERE) for a in arrays]
    return kernel_call(kernel, 1, scalars, blocks, args + sums, outs, stage + scratch, waits, aliases, flops)


def halo_kernel(scalars, tok, cot, w_qkv, w_out, lat, lon, cor, weights, first_x, first_g, strips, w, sems):
    core = scalars[2]
    copies = [
        pltpu.make_async_copy(w_qkv, w, sems.at[0]),
        pltpu.make_async_copy(w_out, weights.at[384:512], sems.at[1]),
    ]
    for n, ref in enumerate((tok, cot)):
        for m, (source, at, rows) in enumerate(
            ((0, 0, 3), (3 + 6 * core, 3, 6), (15 + 6 * core, 9, 3), (18 + 3 * core, 12, 3))
        ):
            copies.append(
                pltpu.make_async_copy(
                    ref.at[:, pl.ds(source, rows), 0:16, :], strips.at[n, :, at : at + rows], sems.at[2 + 5 * n + m]
                )
            )
        columns = pl.ds(pl.multiple_of(16 * core, 16), 32)
        copies.append(
            pltpu.make_async_copy(
                ref.at[:, 0:3, columns, :], lat.at[2 * n : 2 * n + 2], sems.at[6 + 5 * n]
            )
        )
    for n, (ref, first) in enumerate(((tok, first_x), (cot, first_g))):
        copies.append(pltpu.make_async_copy(ref.at[:, pl.ds(3 + 12 * core, 6)], first, sems.at[12 + n]))
    for copy in copies:
        copy.start()
    copies[0].wait()
    for t in range(3):
        weights[128 * t : 128 * t + 128, :] = w[t].T
    for copy in copies[1:]:
        copy.wait()
    for n in range(2):
        strip = strips[n].astype(F32)[:, :, 0:8].astype(BF)
        cor[2 * n : 2 * n + 2] = strip[:, 0:3]
        lon[2 * n : 2 * n + 2] = strip[:, 3:15]


def early_kernel(scalars, half0, half1, other0, other1, out):
    for group, (half, other) in enumerate(((half0, other0), (half1, other1))):
        out[group] = (half[0].astype(F32) + other[0].astype(F32)).astype(BF)


def late_kernel(scalars, half2, half3, other2, other3, out, lat, lon, cor):
    corner = scalars[2] == 1
    for n in range(2):
        row = half2[0, n].astype(F32) + other2[0, n].astype(F32)
        column = half3[0, n].astype(F32) + other3[0, n].astype(F32)
        out[0, n] = row.astype(BF)
        out[1, n] = column.astype(BF)
        if n == 1:
            row = jnp.where(corner, column, row)
            cor[...] = column[:96].reshape(2, 6, 8, D)[:, 3:6].reshape(48, D).astype(BF)
        edge = row.reshape(3, 6, 8, D)[:, 3:6].reshape(72, D)
        lat[n] = jnp.concatenate([edge, jnp.zeros((8, D), F32)], 0).astype(BF)
        lon[n] = column[:96].astype(BF)


def join_kernel(scalars, lat, lon, cor, out):
    out[0:80] = lat[0]
    out[80:160] = lat[1]
    out[160:256] = lon[0]
    out[256:352] = lon[1]
    out[352:400] = cor[...]


def pack_kernel(scalars, payload, first, second, small, small_theirs, out):
    share = out.shape[0]
    other = jnp.concatenate([first[...], second[...]], 0).astype(F32)
    rows = (payload[...] + other).reshape(share, 2048 // share, 128)
    small = small[...] + small_theirs[...]
    high = small.astype(BF).astype(F32)
    pair = jnp.concatenate([high[:, None], (small - high)[:, None], jnp.zeros((8, 6, 128), F32)], 1)
    ride = jnp.concatenate([pair, jnp.zeros((share - 8, 8, 128), F32)], 0)
    out[...] = jnp.concatenate([rows, ride], 1).astype(BF)


def copy_kernel(scalars, a, out):
    out[...] = a[...]


def sum_kernel(scalars, parts, out):
    out[...] = jnp.sum(parts[...].astype(F32), axis=0)


def spread_kernel(scalars, a, b, out):
    total = a[...] + b[...]
    rows = total.shape[0] - 8
    extra = total[rows : rows + 1] + total[rows + 1 : rows + 2]
    high = extra.astype(BF).astype(F32)
    total = jnp.concatenate([total[:rows], high, extra - high, jnp.zeros((6, 128), F32)], 0)
    out[...] = jnp.broadcast_to(total.astype(BF)[None], out.shape)


def small_kernel(scalars, parts, small):
    rows = parts.shape[1] - 8
    values = parts[0:8].astype(F32)
    small[...] = values[:, rows] + values[:, rows + 1]


def unpack_kernel(scalars, parts, gq, go):
    values = parts[...].astype(F32)
    rows = values.shape[1] - 8
    rows = values[:, :rows].reshape(2048, 128)
    for t in range(3):
        gq[t] = rows[512 * t : 512 * t + 512]
    for n in range(4):
        go[:, 128 * n : 128 * n + 128] = rows[1536 + 128 * n : 1664 + 128 * n]


def tile_kernel(scalars, tok, cot, a0, a1, b0, b1, ha, hb, gain, out, windows, halos, stage):
    step = pl.program_id(0)

    @pl.when(step == 0)
    def _():
        place_windows(scalars, a0, a1, b0, b1, ha, hb, windows, halos, stage)

    x, g = tok[...].astype(F32), cot[...].astype(F32)
    unit, inv_std = normalised(x)
    scaled = stage[:, pl.ds(3 * step, 3), 8:56, :] * gain[...].reshape(1, 1, 1, D)
    mean = jnp.sum(scaled, axis=-1, keepdims=True) * (1.0 / D)
    along = jnp.sum(scaled * unit, axis=-1, keepdims=True) * (1.0 / D)
    out[...] = (g + inv_std * (scaled - mean - unit * along)).astype(BF)


def place_windows(scalars, a0, a1, b0, b1, ha, hb, windows, halos, stage):
    for n, (early, late, halo) in enumerate(((a0, a1, ha), (b0, b1, hb))):
        windows[n, 0:2] = early[...]
        windows[n, 2:4] = late[...]
        halos[n] = halo[...]
    core = scalars[2]

    def holder(j):
        return jnp.where(core == j % 2, 0, 1)

    for j in range(4):
        at = 80 * (j % 2)
        edge = halos[holder(j // 2), at : at + 80, :].astype(F32)[:72].reshape(3, 3, 8, D)
        column = 14 + 12 * j
        wide, narrow = (0, 8) if j < 3 else (4, 0)
        stage[:, 0:3, column + wide : column + wide + 8, :] = edge[0:2]
        stage[0, 0:3, column + narrow : column + narrow + 4, :] = edge[2, :, 0:4]
        stage[1, 0:3, column + narrow : column + narrow + 4, :] = edge[2, :, 4:8]
        rows = 6 if j < 3 else 3
        at = 160 + 96 * (j // 2)
        strip = halos[holder(j), at : at + 96, :].astype(F32).reshape(2, 6, 8, D)
        stage[:, 3 + 6 * j : 3 + 6 * j + rows, 6:14, :] = strip[:, :rows]
    stage[:, 0:3, 6:14, :] = halos[holder(3), 352:400, :].astype(F32).reshape(2, 3, 8, D)
    for group in range(4):
        for j in range(4):
            row, col = PLACE[group][j]
            rows = 6 if row < 3 else 3
            value = windows[holder(j), group, j // 2].astype(F32)
            full = value[:96].reshape(2, 6, 8, D)[:, :rows]
            rest = value[96:].reshape(6, 8, D)[:rows]
            column = 14 + 12 * col
            wide, narrow = (0, 8) if group < 3 else (4, 0)
            at = slice(3 + 6 * row, 3 + 6 * row + rows)
            stage[:, at, column + wide : column + wide + 8, :] = full
            stage[0, at, column + narrow : column + narrow + 4, :] = rest[:, 0:4]
            stage[1, at, column + narrow : column + narrow + 4, :] = rest[:, 4:8]


def per_device(tokens, cotangent, norm_gain, norm_bias, w_qkv, w_out):
    core = lax.axis_index("tp") % 2
    edge = lax.axis_index("lat") == lax.axis_size("lat") - 1

    def scalars(first, second):
        masked = jnp.stack([edge & first, edge & second])
        return jnp.concatenate([jnp.where(masked, 1, 0), core.reshape(1)]).astype(jnp.int32)

    never = core < 0
    no_mask, row_mask, column_mask = scalars(never, never), scalars(core >= 0, core == 0), scalars(never, core == 1)

    def swap(block, bit):
        return move(block, ("tp",), lambda t: (t ^ bit,))

    both = (tokens, cotangent)
    h_lat, h_lon, h_cor, mine, *first_rows = kernel_call(
        halo_kernel,
        1,
        no_mask,
        [(a, ANYWHERE) for a in (tokens, cotangent, w_qkv.transpose(1, 0, 2), w_out)],
        [],
        [((4, 3, 32, D), BF), ((4, 12, 8, D), BF), ((4, 3, 8, D), BF), ((512, D), BF)] + [((2, 6, 48, D), BF)] * 2,
        [
            pltpu.VMEM((2, 2, 15, 16, D), BF),
            pltpu.VMEM((3, D, 128), BF),
            pltpu.SemaphoreType.DMA((14,)),
        ],
    )
    theirs = swap(mine, 1)
    h_lat = move(h_lat, ("lat", "tp"), lambda a, t: (a - 1, t ^ 2))
    h_lon = move(h_lon, ("lon",), lambda a: (a - 1,))
    h_cor = move(h_cor, ("lat", "lon"), lambda a, b: (a - 1, b - 1))

    gain = norm_gain.reshape(1, D)
    params = [gain, norm_bias.reshape(1, D), mine, theirs]
    masks = [pltpu.VMEM((2, SPAN, SPAN), F32)]
    half0, *sums, tile_x, tile_g = group_call(
        inner_kernel(0),
        no_mask,
        both,
        first_rows + params,
        [],
        [(t.shape, BF) for t in both],
        (2, 6, 48),
        [pltpu.SemaphoreType.DMA((2, 4))],
        FLOPS[0],
    )
    other0 = swap(half0, 2)
    tiles_in = [tile_x, tile_g]
    half1, *sums = group_call(
        inner_kernel(1), no_mask, [], tiles_in + params, sums, [], (2, 12, 48), [], FLOPS[1]
    )
    other1 = swap(half1, 2)
    half2, *sums = group_call(
        row_kernel, row_mask, [], tiles_in + [h_lat] + params, sums, [], (2, 12, 48), masks, FLOPS[2]
    )
    other2 = swap(half2, 2)
    half3, _, _, _, payload, *payload_theirs, small = group_call(
        column_kernel,
        column_mask,
        [],
        tiles_in + [h_lat, h_lon, h_cor] + params,
        sums,
        [((2048, 128), F32), ((1024, 128), BF), ((1024, 128), BF), ((8, 128), F32)],
        (2, 12, 24),
        masks,
        FLOPS[3],
        [other0],
    )
    other3 = swap(half3, 2)

    lats, lons = lax.axis_size("lat"), lax.axis_size("lon")
    tiles = lats // 2 * lons
    shares = ((tiles, 2048 // tiles + 8, 128), BF)
    groups = [[a * lons + b for a in range(half, lats, 2) for b in range(lons)] for half in range(2)]

    def exchange(block):
        return lax.all_to_all(block, ("lat", "lon"), 0, 0, axis_index_groups=groups, tiled=True)

    small = kernel_call(copy_kernel, 1, no_mask, [], [small], ((8, 128), F32), (), [other1])
    packed = kernel_call(
        pack_kernel, 1, no_mask, [], [payload, *(swap(p, 1) for p in payload_theirs), small, swap(small, 1)], shares, (), [other2]
    )
    parts = exchange(packed)

    early = kernel_call(
        early_kernel,
        1,
        no_mask,
        [(a, whole(a.shape)) for a in (half0, half1)],
        [other0, other1],
        ((2, 2, SPAN, D), BF),
    )
    late, lat_edge, lon_edge, cor_edge = kernel_call(
        late_kernel,
        1,
        no_mask,
        [(a, whole(a.shape)) for a in (half2, half3)],
        [other2, other3],
        [((2, 2, SPAN, D), BF), ((2, 80, D), BF), ((2, 96, D), BF), ((48, D), BF)],
        flops=FLOPS[4],
    )
    lat_edge = move(lat_edge, ("lat", "tp"), lambda a, t: (a + 1, t ^ 2))
    lon_edge = move(lon_edge, ("lon",), lambda a: (a + 1,))
    cor_edge = move(cor_edge, ("lat", "lon"), lambda a, b: (a + 1, b + 1))
    edges = kernel_call(join_kernel, 1, no_mask, [], [lat_edge, lon_edge, cor_edge], ((400, D), BF))
    total = kernel_call(sum_kernel, 1, no_mask, [], [parts], (shares[0][1:], F32))
    other = move(total, ("lat",), lambda a: (a ^ 1,))
    spread = kernel_call(spread_kernel, 1, no_mask, [], [total, other], shares, (), [edges, early])
    gathered = exchange(spread)
    rows = pl.BlockSpec((2, 3, 48, D), lambda i, scalars: (0, i, 0, 0))
    grad_tokens = kernel_call(
        tile_kernel,
        8,
        no_mask,
        [(tokens, rows), (cotangent, rows)],
        [early, late, swap(early, 1), swap(late, 1), edges, swap(edges, 1), gain],
        (tokens.shape, BF, rows),
        [
            pltpu.VMEM((2, 4, 2, SPAN, D), BF),
            pltpu.VMEM((2, 400, D), BF),
            pltpu.VMEM((2, 24, 64, D), F32),
        ],
    )
    tokens_done = pltpu.with_memory_space_constraint(grad_tokens, pltpu.HBM)
    small = kernel_call(small_kernel, 1, no_mask, [], [gathered], ((8, 128), F32), (), [tokens_done])
    small_y = swap(small, 2)
    grad_qkv, grad_out = kernel_call(
        unpack_kernel,
        1,
        no_mask,
        [],
        [gathered],
        [((3, D, 128), F32, whole((3, D, 128))), ((128, D), F32, whole((128, D)))],
        (),
        [small],
    )
    small = small + small_y
    small = small.reshape(2, D)
    return (grad_tokens, small[0], small[1], grad_qkv.transpose(1, 0, 2), grad_out)


def solution(mesh):
    return jax.shard_map(
        per_device,
        mesh=mesh,
        in_specs=(
            P(None, "lat", "lon", None),
            P(None, "lat", "lon", None),
            P(),
            P(),
            P(None, None, "tp"),
            P("tp", None),
        ),
        out_specs=(P(None, "lat", "lon", None), P(), P(), P(None, None, "tp"), P("tp", None)),
        check_vma=False,
    )
```

profile of v0, /device:TPU:32, one launch (start us, length us, event | category | flops | bytes accessed | tf_op | source)
XLA Modules:
  0.0 105.0 jit_solution(17598804048968315992)
XLA Ops:
  0.6 0.1 add_select_fusion
  0.7 0.1 pad_add_fusion.refs_0_
  0.8 3.4 %shard_map.101 = (bf16[4,3,32,512]{3,2,1,0:T(8,128)(2,1)}, bf16[4,12,8,512]{3,2,1,0:T(8,128)(2,1)}, bf16[4,3,8,512]{3,2,1,0:T(8,128)(2,1)}, bf16[512,512]{1,0:T(...) custom-call(s32[3]{0:T(128)S(1)} %pad_add_fusion.refs_0_, ...), custom_call_target="tpu_custom_call" | custom-call | flops 5000000 | bytes 1000000 | tf_op jit(solution)/shard_map/pallas_call | solution.py:286
  4.2 0.1 collective-permute-start
  4.3 5.3 %collective-permute-start.3 = (bf16[4,3,32,512]{3,2,1,0:T(8,128)(2,1)}, bf16[4,3,32,512]{3,2,1,0:T(8,128)(2,1)S(1)}, u32[]{:S(2)}, u32[]{:S(2)}) collective-permute-start(bf16[4,3,32,512]{3,2,1,0:T(8,128)(2,1)} %get-tuple-element.46), channel_id=1, source_target_pairs={{0,226},{1,227},{2,224},{3,225},{32,2},{33,3},{34,0},{35,1},{64,34... | collective-permute-start | bytes 1179656 | tf_op jit(solution)/shard_map/ppermute | solution.py:54
  9.6 0.1 collective-permute-start.4
  9.7 5.9 %collective-permute-start.5 = (bf16[4,3,8,512]{3,2,1,0:T(8,128)(2,1)}, bf16[4,3,8,512]{3,2,1,0:T(8,128)(2,1)S(1)}, u32[]{:S(2)}, u32[]{:S(2)}) collective-permute-start(bf16[4,3,8,512]{3,2,1,0:T(8,128)(2,1)} %get-tuple-element.52), channel_id=1, source_target_pairs={{0,252},{4,224},{8,228},{12,232},{16,236},{20,240},{24,244},{28,24... | collective-permute-start | bytes 294920 | tf_op jit(solution)/shard_map/ppermute | solution.py:54
  15.7 0.1 add_select_fusion.1
  15.7 4.9 %shard_map.102 = (bf16[1,2,144,512]{3,2,1,0:T(8,128)(2,1)}, f32[512,512]{1,0:T(8,128)S(1)}, f32[512,512]{1,0:T(8,128)S(1)}, f32[16,512]{1,0:T(8,128)S(1)}, bf16[...) custom-call(s32[3]{0:T(128)S(1)} %pad_add_fusion.refs_0_, bf16[2,24,48,512]{3,2,1,0:T(8,128)(2,1)} %refs_1_.5, ...), custom_call_target="tpu_custom_call" | custom-call | flops 4000000000 | bytes 1000000 | tf_op jit(solution)/shard_map/pallas_call | solution.py:286
  20.7 0.5 collective-permute-start.1
  21.3 0.1 add_select_fusion.2
  21.4 4.9 %shard_map.103 = (bf16[1,2,144,512]{3,2,1,0:T(8,128)(2,1)}, f32[512,512]{1,0:T(8,128)S(1)}, f32[512,512]{1,0:T(8,128)S(1)}, f32[16,512]{1,0:T(8,128)S(1)}) custom-call(s32[3]{0:T(128)S(1)} %pad_add_fusion.refs_0_, bf16[2,24,48,512]{3,2,1,0:T(8,128)(2,1)S(1)} %get-tuple-element.40.refs_1_, ...), custom_call_target="tpu_custom_call", output_to_operand_aliasing={{1}: (7, {}), {2}: (8, {}), {3}: (9, {})} | custom-call | flops 50000000 | bytes 1000000 | tf_op jit(solution)/shard_map/pallas_call | solution.py:286
  26.2 1.6 %collective-permute-start.2 = (bf16[1,2,144,512]{3,2,1,0:T(8,128)(2,1)}, bf16[1,2,144,512]{3,2,1,0:T(8,128)(2,1)S(1)}, u32[]{:S(2)}, u32[]{:S(2)}) collective-permute-start(bf16[1,2,144,512]{3,2,1,0:T(8,128)(2,1)} %get-tuple-element.45.refs_2_), channel_id=1, source_target_pairs={{0,2},{1,3},{2,0},{3,1},{4,6},{5,7},{6,4},{7,5},{8,10},{9,11},{10,... | collective-permute-start | bytes 884744 | tf_op jit(solution)/shard_map/ppermute | solution.py:54
  27.8 5.1 %shard_map.105 = (bf16[1,2,144,512]{3,2,1,0:T(8,128)(2,1)}, f32[512,512]{1,0:T(8,128)S(1)}, f32[512,512]{1,0:T(8,128)S(1)}, f32[16,512]{1,0:T(8,128)S(1)}) custom-call(s32[3]{0:T(128)S(1)} %pad_add_fusion.1.refs_0_, bf16[2,24,48,512]{3,2,1,0:T(8,128)(2,1)S(1)} %get-tuple-element.40.refs_1_, ...), custom_call_target="tpu_custom_call", output_to_operand_aliasing={{1}: (8, {}), {2}: (9, {}), {3}: (10, {})} | custom-call | flops 50000000 | bytes 1000000 | tf_op jit(solution)/shard_map/pallas_call | solution.py:286
  32.9 0.4 collective-permute-start.6
  33.4 4.8 %shard_map.106 = (bf16[1,2,144,512]{3,2,1,0:T(8,128)(2,1)}, f32[512,512]{1,0:T(8,128)S(1)}, f32[512,512]{1,0:T(8,128)S(1)}, f32[16,512]{1,0:T(8,128)S(1)}, f32[2...) custom-call(s32[3]{0:T(128)S(1)} %pad_add_fusion.2.refs_0_, ...), custom_call_target="tpu_custom_call", output_to_operand_aliasing={{1}: (10, {}), {2}: (11, {}), {3}: (12, {})} | custom-call | flops 50000000 | bytes 1000000 | tf_op jit(solution)/shard_map/pallas_call | solution.py:286
  38.2 0.5 collective-permute-start.15
  38.7 1.6 %collective-permute-start.7 = (bf16[1,2,144,512]{3,2,1,0:T(8,128)(2,1)}, bf16[1,2,144,512]{3,2,1,0:T(8,128)(2,1)S(1)}, u32[]{:S(2)}, u32[]{:S(2)}) collective-permute-start(bf16[1,2,144,512]{3,2,1,0:T(8,128)(2,1)} %get-tuple-element.56.refs_2_), channel_id=1, source_target_pairs={{0,2},{1,3},{2,0},{3,1},{4,6},{5,7},{6,4},{7,5},{8,10},{9,11},{10,... | collective-permute-start | bytes 884744 | tf_op jit(solution)/shard_map/ppermute | solution.py:54
  40.3 0.5 shard_map.110.refs_4_
  40.8 0.1 collective-permute-start.16
  40.9 1.7 %collective-permute-done.6.refs_3_.refs_6_ = bf16[1,2,144,512]{3,2,1,0:T(8,128)(2,1)S(1)} collective-permute-done((bf16[1,2,144,512]{3,2,1,0:T(8,128)(2,1)}, bf16[1,2,144,512]{3,2,1,0:T(8,128)(2,1)S(1)}, u32[]{:S(2)}, u32[]{:S(2)}) %collective-permute-start.6) | collective-permute-done | bytes 294944 | tf_op jit(solution)/shard_map/ppermute | solution.py:54
  42.7 1.5 %shard_map.111 = bf16[32,72,128]{2,1,0:T(8,128)(2,1)} custom-call(s32[3]{0:T(128)S(1)} %pad_add_fusion.refs_0_, f32[2048,128]{1,0:T(8,128)S(1)} %get-tuple-element.61.refs_1_, bf16[1024,128]{1,0:T(8,128)(2,1)S(1)} %collective-permute-done.14.refs_2_, bf16[1024,128]{1,0:T(8,128)(2,1)S(1)} %collective-permute-done.15.refs_3_, ...), custom_call_target="tpu_custom_call" | custom-call | flops 5000000 | bytes 1000000 | tf_op jit(solution)/shard_map/pallas_call | solution.py:286
  44.2 7.1 %all-to-all-start = ((bf16[32,72,128]{2,1,0:T(8,128)(2,1)}), bf16[32,72,128]{2,1,0:T(8,128)(2,1)S(1)}, u32[]{:S(2)}, u32[]{:S(2)}) async-start(bf16[32,72,128]{2,1,0:T(8,128)(2,1)} %shard_map.111), calls=%async_computation | async-start | bytes 1179648 | tf_op jit(solution)/shard_map/all_to_all | solution.py:560
  51.3 1.7 %shard_map.107 = (bf16[2,2,144,512]{3,2,1,0:T(8,128)(2,1)S(1)}, bf16[2,80,512]{2,1,0:T(8,128)(2,1)S(1)}, bf16[2,96,512]{2,1,0:T(8,128)(2,1)S(1)}, bf16[48,512]{1,0:T(8,128)(2,1)S(1)}) custom-call(s32[3]{0:T(128)S(1)} %pad_add_fusion.refs_0_, bf16[1,2,144,512]{3,2,1,0:T(8,128)(2,1)} %get-tuple-element.50.refs_1_, ...), custom_call_target="tpu_custom_call" | custom-call | flops 8000000000 | bytes 1000000 | tf_op jit(solution)/shard_map/pallas_call | solution.py:286
  53.1 1.5 %collective-permute-start.11 = (bf16[2,96,512]{2,1,0:T(8,128)(2,1)S(1)}, bf16[2,96,512]{2,1,0:T(8,128)(2,1)S(1)}, u32[]{:S(2)}, u32[]{:S(2)}) collective-permute-start(bf16[2,96,512]{2,1,0:T(8,128)(2,1)S(1)} %get-tuple-element.59), channel_id=1, source_target_pairs={{0,4},{4,8},{8,12},{12,16},{16,20},{20,24},{24,28},{28,0},{1,5},{5... | collective-permute-start | bytes 589832 | tf_op jit(solution)/shard_map/ppermute | solution.py:54
  54.6 1.4 %collective-permute-start.10 = (bf16[2,80,512]{2,1,0:T(8,128)(2,1)S(1)}, bf16[2,80,512]{2,1,0:T(8,128)(2,1)S(1)}, u32[]{:S(2)}, u32[]{:S(2)}) collective-permute-start(bf16[2,80,512]{2,1,0:T(8,128)(2,1)S(1)} %get-tuple-element.58), channel_id=1, source_target_pairs={{0,34},{1,35},{2,32},{3,33},{32,66},{33,67},{34,64},{35,65},{64,98... | collective-permute-start | bytes 491528 | tf_op jit(solution)/shard_map/ppermute | solution.py:54
  56.0 3.0 %collective-permute-start.12 = (bf16[48,512]{1,0:T(8,128)(2,1)S(1)}, bf16[48,512]{1,0:T(8,128)(2,1)S(1)}, u32[]{:S(2)}, u32[]{:S(2)}) collective-permute-start(bf16[48,512]{1,0:T(8,128)(2,1)S(1)} %get-tuple-element.60), channel_id=1, source_target_pairs={{0,36},{4,40},{8,44},{12,48},{16,52},{20,56},{24,60},{28,32},{32,6... | collective-permute-start | bytes 147464 | tf_op jit(solution)/shard_map/ppermute | solution.py:54
  58.9 10.5 %all-to-all-done.refs_1_ = bf16[32,72,128]{2,1,0:T(8,128)(2,1)S(1)} async-done(((bf16[32,72,128]{2,1,0:T(8,128)(2,1)}), bf16[32,72,128]{2,1,0:T(8,128)(2,1)S(1)}, u32[]{:S(2)}, u32[]{:S(2)}) %all-to-all-start) | async-done | bytes 589856 | tf_op jit(solution)/shard_map/all_to_all | solution.py:560
  69.5 0.6 shard_map.112.refs_1_
  70.1 3.2 %collective-permute-start.17 = (f32[72,128]{1,0:T(8,128)S(1)}, f32[72,128]{1,0:T(8,128)S(1)}, u32[]{:S(2)}, u32[]{:S(2)}) collective-permute-start(f32[72,128]{1,0:T(8,128)S(1)} %shard_map.112.refs_1_), channel_id=1, source_target_pairs={{0,32},{32,0},{64,96},{96,64},{128,160},{160,128},{192,224},{224,1... | collective-permute-start | bytes 110600 | tf_op jit(solution)/shard_map/ppermute | solution.py:54
  73.3 1.7 %shard_map.104.refs_3_.refs_4_ = bf16[2,2,144,512]{3,2,1,0:T(8,128)(2,1)S(1)} custom-call(s32[3]{0:T(128)S(1)} %pad_add_fusion.refs_0_, bf16[1,2,144,512]{3,2,1,0:T(8,128)(2,1)} %get-tuple-element.39.refs_1_, bf16[1,2,144,512]{3,2,1,0:T(8,128)(2,1)} %get-tuple-element.45.refs_2_, bf16[1,2,144,512]{3,2,1,0:T(8,128)(2,1)S(1)} %collective-permute-done.1.refs_3_.refs_13_, ...), custom_call_target="tpu_custom_call" | custom-call | flops 5000000 | bytes 1000000 | tf_op jit(solution)/shard_map/pallas_call | solution.py:286
  75.0 0.6 shard_map.108.refs_7_.refs_3_
  75.6 0.3 collective-permute-done.17.refs_2_
  75.9 1.4 %shard_map.113 = bf16[32,72,128]{2,1,0:T(8,128)(2,1)} custom-call(s32[3]{0:T(128)S(1)} %pad_add_fusion.refs_0_, f32[72,128]{1,0:T(8,128)S(1)} %shard_map.112.refs_1_, f32[72,128]{1,0:T(8,128)S(1)} %collective-permute-done.17.refs_2_, bf16[400,512]{1,0:T(8,128)(2,1)S(1)} %shard_map.108.refs_7_.refs_3_, bf16[2,2,144,512]{3,2,1,0:T(8,128)(2,1)S(1)} %shard_map.104.refs_3_.refs_4_), custom_call_target="tpu_custom_call" | custom-call | flops 5000000 | bytes 1000000 | tf_op jit(solution)/shard_map/pallas_call | solution.py:286
  77.3 5.2 %all-to-all-start.1 = ((bf16[32,72,128]{2,1,0:T(8,128)(2,1)}), bf16[32,72,128]{2,1,0:T(8,128)(2,1)S(1)}, u32[]{:S(2)}, u32[]{:S(2)}) async-start(bf16[32,72,128]{2,1,0:T(8,128)(2,1)} %shard_map.113), calls=%async_computation.1 | async-start | bytes 1179648 | tf_op jit(solution)/shard_map/all_to_all | solution.py:560
  82.5 0.1 collective-permute-start.8
  82.6 0.5 collective-permute-start.9
  83.1 0.1 collective-permute-start.13
  83.2 1.4 %collective-permute-done.8.refs_5_ = bf16[2,2,144,512]{3,2,1,0:T(8,128)(2,1)S(1)} collective-permute-done((bf16[2,2,144,512]{3,2,1,0:T(8,128)(2,1)S(1)}, bf16[2,2,144,512]{3,2,1,0:T(8,128)(2,1)S(1)}, u32[]{:S(2)}, u32[]{:S(2)}) %collective-permute-start.8) | collective-permute-done | bytes 589856 | tf_op jit(solution)/shard_map/ppermute | solution.py:54
  84.6 0.8 collective-permute-done.9.refs_6_
  85.4 0.6 collective-permute-done.13.refs_8_
  86.0 9.2 %shard_map.109.refs_2_ = bf16[2,24,48,512]{3,2,1,0:T(8,128)(2,1)} custom-call(s32[3]{0:T(128)S(1)} %pad_add_fusion.refs_0_, bf16[2,24,48,512]{3,2,1,0:T(8,128)(2,1)} %refs_1_.5, bf16[2,24,48,512]{3,2,1,0:T(8,128)(2,1)} %refs_2_.5, bf16[2,2,144,512]{3,2,1,0:T(8,128)(2,1)S(1)} %shard_map.104.refs_3_.refs_4_, ...), custom_call_target="tpu_custom_call" | custom-call | flops 5000000 | bytes 1000000 | tf_op jit(solution)/shard_map/pallas_call | solution.py:286
  95.3 4.9 %all-to-all-done.1.refs_1_ = bf16[32,72,128]{2,1,0:T(8,128)(2,1)S(1)} async-done(((bf16[32,72,128]{2,1,0:T(8,128)(2,1)}), bf16[32,72,128]{2,1,0:T(8,128)(2,1)S(1)}, u32[]{:S(2)}, u32[]{:S(2)}) %all-to-all-start.1) | async-done | bytes 589856 | tf_op jit(solution)/shard_map/all_to_all | solution.py:560
  100.2 0.5 shard_map.114.refs_2_
  100.7 0.2 collective-permute-start.18
  100.9 1.6 %shard_map.115 = (f32[3,512,128]{2,1,0:T(8,128)}, f32[128,512]{1,0:T(8,128)}) custom-call(s32[3]{0:T(128)S(1)} %pad_add_fusion.refs_0_, bf16[32,72,128]{2,1,0:T(8,128)(2,1)S(1)} %all-to-all-done.1.refs_1_, f32[8,128]{1,0:T(8,128)S(1)} %shard_map.114.refs_2_), custom_call_target="tpu_custom_call" | custom-call | flops 5000000 | bytes 1000000 | tf_op jit(solution)/shard_map/pallas_call | solution.py:286
  102.5 2.0 %collective-permute-done.18 = f32[8,128]{1,0:T(8,128)S(1)} collective-permute-done((f32[8,128]{1,0:T(8,128)S(1)}, f32[8,128]{1,0:T(8,128)S(1)}, u32[]{:S(2)}, u32[]{:S(2)}) %collective-permute-start.18) | collective-permute-done | bytes 4128 | tf_op jit(solution)/shard_map/ppermute | solution.py:54
  104.4 0.6 slice_bitcast_fusion
  (21 shorter events, 0.2 us)
Async XLA Ops:
  0.8 14.9 %copy-start = (f32[512]{0:T(512)S(1)}, f32[512]{0:T(512)}, u32[]{:S(2)}) copy-start(f32[512]{0:T(512)} %param.8) | copy-start | bytes 6148
  0.8 14.9 %copy-start.1 = (f32[512]{0:T(512)S(1)}, f32[512]{0:T(512)}, u32[]{:S(2)}) copy-start(f32[512]{0:T(512)} %param.9) | copy-start | bytes 6148
  4.2 11.5 %collective-permute-start = (bf16[512,512]{1,0:T(8,128)(2,1)S(1)}, bf16[512,512]{1,0:T(8,128)(2,1)S(1)}, u32[]{:S(2)}, u32[]{:S(2)}) collective-permute-start(bf16[512,512]{1,0:T(8,128)(2,1)S(1)} %get-tuple-element.38.refs_7_.refs_5_.refs_6_.refs_8_), channel_id=1, source_target_pairs={{0,1},{1,0},{2,3},{3,2},{4,5},{5,4},{6,7},{7,6},{8,9},{9,8},{10,11... | collective-permute-start | bytes 1572872 | tf_op jit(solution)/shard_map/ppermute | solution.py:54
  4.3 23.5 %collective-permute-start.3 = (bf16[4,3,32,512]{3,2,1,0:T(8,128)(2,1)}, bf16[4,3,32,512]{3,2,1,0:T(8,128)(2,1)S(1)}, u32[]{:S(2)}, u32[]{:S(2)}) collective-permute-start(bf16[4,3,32,512]{3,2,1,0:T(8,128)(2,1)} %get-tuple-element.46), channel_id=1, source_target_pairs={{0,226},{1,227},{2,224},{3,225},{32,2},{33,3},{34,0},{35,1},{64,34... | collective-permute-start | bytes 1179656 | tf_op jit(solution)/shard_map/ppermute | solution.py:54
  9.6 23.8 %collective-permute-start.4 = (bf16[4,12,8,512]{3,2,1,0:T(8,128)(2,1)}, bf16[4,12,8,512]{3,2,1,0:T(8,128)(2,1)S(1)}, u32[]{:S(2)}, u32[]{:S(2)}) collective-permute-start(bf16[4,12,8,512]{3,2,1,0:T(8,128)(2,1)} %get-tuple-element.51), channel_id=1, source_target_pairs={{0,28},{4,0},{8,4},{12,8},{16,12},{20,16},{24,20},{28,24},{1,29},{... | collective-permute-start | bytes 1179656 | tf_op jit(solution)/shard_map/ppermute | solution.py:54
  9.7 23.7 %collective-permute-start.5 = (bf16[4,3,8,512]{3,2,1,0:T(8,128)(2,1)}, bf16[4,3,8,512]{3,2,1,0:T(8,128)(2,1)S(1)}, u32[]{:S(2)}, u32[]{:S(2)}) collective-permute-start(bf16[4,3,8,512]{3,2,1,0:T(8,128)(2,1)} %get-tuple-element.52), channel_id=1, source_target_pairs={{0,252},{4,224},{8,228},{12,232},{16,236},{20,240},{24,244},{28,24... | collective-permute-start | bytes 294920 | tf_op jit(solution)/shard_map/ppermute | solution.py:54
  20.7 12.8 %collective-permute-start.1 = (bf16[1,2,144,512]{3,2,1,0:T(8,128)(2,1)}, bf16[1,2,144,512]{3,2,1,0:T(8,128)(2,1)S(1)}, u32[]{:S(2)}, u32[]{:S(2)}) collective-permute-start(bf16[1,2,144,512]{3,2,1,0:T(8,128)(2,1)} %get-tuple-element.39.refs_1_), channel_id=1, source_target_pairs={{0,2},{1,3},{2,0},{3,1},{4,6},{5,7},{6,4},{7,5},{8,10},{9,11},{10,... | collective-permute-start | bytes 884744 | tf_op jit(solution)/shard_map/ppermute | solution.py:54
  26.2 14.1 %collective-permute-start.2 = (bf16[1,2,144,512]{3,2,1,0:T(8,128)(2,1)}, bf16[1,2,144,512]{3,2,1,0:T(8,128)(2,1)S(1)}, u32[]{:S(2)}, u32[]{:S(2)}) collective-permute-start(bf16[1,2,144,512]{3,2,1,0:T(8,128)(2,1)} %get-tuple-element.45.refs_2_), channel_id=1, source_target_pairs={{0,2},{1,3},{2,0},{3,1},{4,6},{5,7},{6,4},{7,5},{8,10},{9,11},{10,... | collective-permute-start | bytes 884744 | tf_op jit(solution)/shard_map/ppermute | solution.py:54
  32.9 9.8 %collective-permute-start.6 = (bf16[1,2,144,512]{3,2,1,0:T(8,128)(2,1)}, bf16[1,2,144,512]{3,2,1,0:T(8,128)(2,1)S(1)}, u32[]{:S(2)}, u32[]{:S(2)}) collective-permute-start(bf16[1,2,144,512]{3,2,1,0:T(8,128)(2,1)} %get-tuple-element.50.refs_1_), channel_id=1, source_target_pairs={{0,2},{1,3},{2,0},{3,1},{4,6},{5,7},{6,4},{7,5},{8,10},{9,11},{10,... | collective-permute-start | bytes 884744 | tf_op jit(solution)/shard_map/ppermute | solution.py:54
  38.2 4.5 %collective-permute-start.14 = (bf16[1024,128]{1,0:T(8,128)(2,1)S(1)}, bf16[1024,128]{1,0:T(8,128)(2,1)S(1)}, u32[]{:S(2)}, u32[]{:S(2)}) collective-permute-start(bf16[1024,128]{1,0:T(8,128)(2,1)S(1)} %get-tuple-element.62), channel_id=1, source_target_pairs={{0,1},{1,0},{2,3},{3,2},{4,5},{5,4},{6,7},{7,6},{8,9},{9,8},{10,11... | collective-permute-start | bytes 786440 | tf_op jit(solution)/shard_map/ppermute | solution.py:54
  38.2 4.5 %collective-permute-start.15 = (bf16[1024,128]{1,0:T(8,128)(2,1)S(1)}, bf16[1024,128]{1,0:T(8,128)(2,1)S(1)}, u32[]{:S(2)}, u32[]{:S(2)}) collective-permute-start(bf16[1024,128]{1,0:T(8,128)(2,1)S(1)} %get-tuple-element.63), channel_id=1, source_target_pairs={{0,1},{1,0},{2,3},{3,2},{4,5},{5,4},{6,7},{7,6},{8,9},{9,8},{10,11... | collective-permute-start | bytes 786440 | tf_op jit(solution)/shard_map/ppermute | solution.py:54
  38.7 12.6 %collective-permute-start.7 = (bf16[1,2,144,512]{3,2,1,0:T(8,128)(2,1)}, bf16[1,2,144,512]{3,2,1,0:T(8,128)(2,1)S(1)}, u32[]{:S(2)}, u32[]{:S(2)}) collective-permute-start(bf16[1,2,144,512]{3,2,1,0:T(8,128)(2,1)} %get-tuple-element.56.refs_2_), channel_id=1, source_target_pairs={{0,2},{1,3},{2,0},{3,1},{4,6},{5,7},{6,4},{7,5},{8,10},{9,11},{10,... | collective-permute-start | bytes 884744 | tf_op jit(solution)/shard_map/ppermute | solution.py:54
  40.8 1.8 %collective-permute-start.16 = (f32[8,128]{1,0:T(8,128)S(1)}, f32[8,128]{1,0:T(8,128)S(1)}, u32[]{:S(2)}, u32[]{:S(2)}) collective-permute-start(f32[8,128]{1,0:T(8,128)S(1)} %shard_map.110.refs_4_), channel_id=1, source_target_pairs={{0,1},{1,0},{2,3},{3,2},{4,5},{5,4},{6,7},{7,6},{8,9},{9,8},{10,11... | collective-permute-start | bytes 12296 | tf_op jit(solution)/shard_map/ppermute | solution.py:54
  44.2 25.3 %all-to-all-start = ((bf16[32,72,128]{2,1,0:T(8,128)(2,1)}), bf16[32,72,128]{2,1,0:T(8,128)(2,1)S(1)}, u32[]{:S(2)}, u32[]{:S(2)}) async-start(bf16[32,72,128]{2,1,0:T(8,128)(2,1)} %shard_map.111), calls=%async_computation | async-start | bytes 1179648 | tf_op jit(solution)/shard_map/all_to_all | solution.py:560
  53.1 21.9 %collective-permute-start.11 = (bf16[2,96,512]{2,1,0:T(8,128)(2,1)S(1)}, bf16[2,96,512]{2,1,0:T(8,128)(2,1)S(1)}, u32[]{:S(2)}, u32[]{:S(2)}) collective-permute-start(bf16[2,96,512]{2,1,0:T(8,128)(2,1)S(1)} %get-tuple-element.59), channel_id=1, source_target_pairs={{0,4},{4,8},{8,12},{12,16},{16,20},{20,24},{24,28},{28,0},{1,5},{5... | collective-permute-start | bytes 589832 | tf_op jit(solution)/shard_map/ppermute | solution.py:54
  54.6 20.4 %collective-permute-start.10 = (bf16[2,80,512]{2,1,0:T(8,128)(2,1)S(1)}, bf16[2,80,512]{2,1,0:T(8,128)(2,1)S(1)}, u32[]{:S(2)}, u32[]{:S(2)}) collective-permute-start(bf16[2,80,512]{2,1,0:T(8,128)(2,1)S(1)} %get-tuple-element.58), channel_id=1, source_target_pairs={{0,34},{1,35},{2,32},{3,33},{32,66},{33,67},{34,64},{35,65},{64,98... | collective-permute-start | bytes 491528 | tf_op jit(solution)/shard_map/ppermute | solution.py:54
  56.0 19.0 %collective-permute-start.12 = (bf16[48,512]{1,0:T(8,128)(2,1)S(1)}, bf16[48,512]{1,0:T(8,128)(2,1)S(1)}, u32[]{:S(2)}, u32[]{:S(2)}) collective-permute-start(bf16[48,512]{1,0:T(8,128)(2,1)S(1)} %get-tuple-element.60), channel_id=1, source_target_pairs={{0,36},{4,40},{8,44},{12,48},{16,52},{20,56},{24,60},{28,32},{32,6... | collective-permute-start | bytes 147464 | tf_op jit(solution)/shard_map/ppermute | solution.py:54
  70.1 5.8 %collective-permute-start.17 = (f32[72,128]{1,0:T(8,128)S(1)}, f32[72,128]{1,0:T(8,128)S(1)}, u32[]{:S(2)}, u32[]{:S(2)}) collective-permute-start(f32[72,128]{1,0:T(8,128)S(1)} %shard_map.112.refs_1_), channel_id=1, source_target_pairs={{0,32},{32,0},{64,96},{96,64},{128,160},{160,128},{192,224},{224,1... | collective-permute-start | bytes 110600 | tf_op jit(solution)/shard_map/ppermute | solution.py:54
  77.3 22.9 %all-to-all-start.1 = ((bf16[32,72,128]{2,1,0:T(8,128)(2,1)}), bf16[32,72,128]{2,1,0:T(8,128)(2,1)S(1)}, u32[]{:S(2)}, u32[]{:S(2)}) async-start(bf16[32,72,128]{2,1,0:T(8,128)(2,1)} %shard_map.113), calls=%async_computation.1 | async-start | bytes 1179648 | tf_op jit(solution)/shard_map/all_to_all | solution.py:560
  82.5 2.1 %collective-permute-start.8 = (bf16[2,2,144,512]{3,2,1,0:T(8,128)(2,1)S(1)}, bf16[2,2,144,512]{3,2,1,0:T(8,128)(2,1)S(1)}, u32[]{:S(2)}, u32[]{:S(2)}) collective-permute-start(bf16[2,2,144,512]{3,2,1,0:T(8,128)(2,1)S(1)} %shard_map.104.refs_3_.refs_4_), channel_id=1, source_target_pairs={{0,1},{1,0},{2,3},{3,2},{4,5},{5,4},{6,7},{7,6},{8,9},{9,8},{10,11... | collective-permute-start | bytes 1769480 | tf_op jit(solution)/shard_map/ppermute | solution.py:54
  82.6 2.8 %collective-permute-start.9 = (bf16[2,2,144,512]{3,2,1,0:T(8,128)(2,1)S(1)}, bf16[2,2,144,512]{3,2,1,0:T(8,128)(2,1)S(1)}, u32[]{:S(2)}, u32[]{:S(2)}) collective-permute-start(bf16[2,2,144,512]{3,2,1,0:T(8,128)(2,1)S(1)} %get-tuple-element.57.refs_4_), channel_id=1, source_target_pairs={{0,1},{1,0},{2,3},{3,2},{4,5},{5,4},{6,7},{7,6},{8,9},{9,8},{10,11... | collective-permute-start | bytes 1769480 | tf_op jit(solution)/shard_map/ppermute | solution.py:54
  83.1 2.9 %collective-permute-start.13 = (bf16[400,512]{1,0:T(8,128)(2,1)S(1)}, bf16[400,512]{1,0:T(8,128)(2,1)S(1)}, u32[]{:S(2)}, u32[]{:S(2)}) collective-permute-start(bf16[400,512]{1,0:T(8,128)(2,1)S(1)} %shard_map.108.refs_7_.refs_3_), channel_id=1, source_target_pairs={{0,1},{1,0},{2,3},{3,2},{4,5},{5,4},{6,7},{7,6},{8,9},{9,8},{10,11... | collective-permute-start | bytes 1228808 | tf_op jit(solution)/shard_map/ppermute | solution.py:54
  100.7 3.7 %collective-permute-start.18 = (f32[8,128]{1,0:T(8,128)S(1)}, f32[8,128]{1,0:T(8,128)S(1)}, u32[]{:S(2)}, u32[]{:S(2)}) collective-permute-start(f32[8,128]{1,0:T(8,128)S(1)} %shard_map.114.refs_2_), channel_id=1, source_target_pairs={{0,2},{1,3},{2,0},{3,1},{4,6},{5,7},{6,4},{7,5},{8,10},{9,11},{10,... | collective-permute-start | bytes 12296 | tf_op jit(solution)/shard_map/ppermute | solution.py:54
where the time goes:
time: 106 us; the launch traced here: 105 us
  Pallas kernels  42.5 us (40%)
  starting transfers between devices  38.4 us (36%)
  waiting for transfers between devices  22.3 us (21%)
    pallas_call x15, Pallas kernels, kernel_call(): pl.pallas_call(body, grid_spec=pltpu.PrefetchScalarGridSpec(num_scalar_pr...  42.5 us
    ppermute x19, starting transfers between devices, move(): lax.ppermute(block, axes, [(i, index(step(*coords(i)))) for i in range(to...  26 us
    all_to_all x2, waiting for transfers between devices, exchange(): lax.all_to_all(block, ('lat', 'lon'), 0, 0, axis_index_groups=groups, til...  15.5 us
    all_to_all x2, starting transfers between devices, exchange(): lax.all_to_all(block, ('lat', 'lon'), 0, 0, axis_index_groups=groups, til...  12.4 us
    ppermute x19, waiting for transfers between devices, move(): lax.ppermute(block, axes, [(i, index(step(*coords(i)))) for i in range(to...  6.84 us
  transfers between devices with their start and end apart: 21, of which 8 were waited for; matrix products, arithmetic and copies ran while one was open for 0% of the time, Pallas kernels for 35%

commit v1 on v0

--- a/solution.py
+++ b/solution.py
@@ -436,7 +436,7 @@
 
     x, g = tok[...].astype(F32), cot[...].astype(F32)
     unit, inv_std = normalised(x)
-    scaled = stage[:, pl.ds(3 * step, 3), 8:56, :] * gain[...].reshape(1, 1, 1, D)
+    scaled = stage[:, pl.ds(6 * step, 6), 8:56, :] * gain[...].reshape(1, 1, 1, D)
     mean = jnp.sum(scaled, axis=-1, keepdims=True) * (1.0 / D)
     along = jnp.sum(scaled * unit, axis=-1, keepdims=True) * (1.0 / D)
     out[...] = (g + inv_std * (scaled - mean - unit * along)).astype(BF)
@@ -590,10 +590,10 @@
     other = move(total, ("lat",), lambda a: (a ^ 1,))
     spread = kernel_call(spread_kernel, 1, no_mask, [], [total, other], shares, (), [edges, early])
     gathered = exchange(spread)
-    rows = pl.BlockSpec((2, 3, 48, D), lambda i, scalars: (0, i, 0, 0))
+    rows = pl.BlockSpec((2, 6, 48, D), lambda i, scalars: (0, i, 0, 0))
     grad_tokens = kernel_call(
         tile_kernel,
-        8,
+        4,
         no_mask,
         [(tokens, rows), (cotangent, rows)],
         [early, late, swap(early, 1), swap(late, 1), edges, swap(edges, 1), gain],

time: 106 us -> 105 us (level)
  Pallas kernels: 42.5 us -> 40.8 us
  waiting for transfers between devices: 22.3 us -> 24 us
    pallas_call x15, Pallas kernels: 42.5 us -> 40.8 us  [kernel_call(): pl.pallas_call(body, grid_spec=pltpu.PrefetchScalarGridSpec(num_scalar_pr...]
    all_to_all x2, waiting for transfers between devices: 15.5 us -> 17.2 us  [exchange(): lax.all_to_all(block, ('lat', 'lon'), 0, 0, axis_index_groups=groups, til...]
  transfers between devices with their start and end apart: 21 -> 21, of which waited for: 8 -> 8; matrix products, arithmetic and copies ran while one was open for 0% -> 0% of each run, Pallas kernels for 35% -> 34%
where the time goes in v1:
time: 105 us
  Pallas kernels  40.8 us (39%)
  starting transfers between devices  38.4 us (37%)
  waiting for transfers between devices  24 us (23%)
    pallas_call x15, Pallas kernels, kernel_call(): pl.pallas_call(body, grid_spec=pltpu.PrefetchScalarGridSpec(num_scalar_pr...  40.8 us
    ppermute x19, starting transfers between devices, move(): lax.ppermute(block, axes, [(i, index(step(*coords(i)))) for i in range(to...  26 us
    all_to_all x2, waiting for transfers between devices, exchange(): lax.all_to_all(block, ('lat', 'lon'), 0, 0, axis_index_groups=groups, til...  17.2 us
    all_to_all x2, starting transfers between devices, exchange(): lax.all_to_all(block, ('lat', 'lon'), 0, 0, axis_index_groups=groups, til...  12.4 us
    ppermute x19, waiting for transfers between devices, move(): lax.ppermute(block, axes, [(i, index(step(*coords(i)))) for i in range(to...  6.84 us
  transfers between devices with their start and end apart: 21, of which 8 were waited for; matrix products, arithmetic and copies ran while one was open for 0% of the time, Pallas kernels for 34%

profile of v1, /device:TPU:32, one launch (start us, length us, event | category | flops | bytes accessed | tf_op | source)
XLA Modules:
  0.0 105.0 jit_solution(17542683598281330722)
XLA Ops:
  0.6 0.1 add_select_fusion
  0.7 0.1 pad_add_fusion.refs_0_
  0.8 3.4 %shard_map.101 = (bf16[4,3,32,512]{3,2,1,0:T(8,128)(2,1)}, bf16[4,12,8,512]{3,2,1,0:T(8,128)(2,1)}, bf16[4,3,8,512]{3,2,1,0:T(8,128)(2,1)}, bf16[512,512]{1,0:T(...) custom-call(s32[3]{0:T(128)S(1)} %pad_add_fusion.refs_0_, ...), custom_call_target="tpu_custom_call" | custom-call | flops 5000000 | bytes 1000000 | tf_op jit(solution)/shard_map/pallas_call | solution.py:286
  4.2 0.1 collective-permute-start
  4.3 5.3 %collective-permute-start.3 = (bf16[4,3,32,512]{3,2,1,0:T(8,128)(2,1)}, bf16[4,3,32,512]{3,2,1,0:T(8,128)(2,1)S(1)}, u32[]{:S(2)}, u32[]{:S(2)}) collective-permute-start(bf16[4,3,32,512]{3,2,1,0:T(8,128)(2,1)} %get-tuple-element.46), channel_id=1, source_target_pairs={{0,226},{1,227},{2,224},{3,225},{32,2},{33,3},{34,0},{35,1},{64,34... | collective-permute-start | bytes 1179656 | tf_op jit(solution)/shard_map/ppermute | solution.py:54
  9.6 0.1 collective-permute-start.4
  9.7 5.9 %collective-permute-start.5 = (bf16[4,3,8,512]{3,2,1,0:T(8,128)(2,1)}, bf16[4,3,8,512]{3,2,1,0:T(8,128)(2,1)S(1)}, u32[]{:S(2)}, u32[]{:S(2)}) collective-permute-start(bf16[4,3,8,512]{3,2,1,0:T(8,128)(2,1)} %get-tuple-element.52), channel_id=1, source_target_pairs={{0,252},{4,224},{8,228},{12,232},{16,236},{20,240},{24,244},{28,24... | collective-permute-start | bytes 294920 | tf_op jit(solution)/shard_map/ppermute | solution.py:54
  15.7 0.1 add_select_fusion.1
  15.7 4.9 %shard_map.102 = (bf16[1,2,144,512]{3,2,1,0:T(8,128)(2,1)}, f32[512,512]{1,0:T(8,128)S(1)}, f32[512,512]{1,0:T(8,128)S(1)}, f32[16,512]{1,0:T(8,128)S(1)}, bf16[...) custom-call(s32[3]{0:T(128)S(1)} %pad_add_fusion.refs_0_, bf16[2,24,48,512]{3,2,1,0:T(8,128)(2,1)} %refs_1_.5, ...), custom_call_target="tpu_custom_call" | custom-call | flops 4000000000 | bytes 1000000 | tf_op jit(solution)/shard_map/pallas_call | solution.py:286
  20.7 0.5 collective-permute-start.1
  21.3 0.1 add_select_fusion.2
  21.4 4.9 %shard_map.103 = (bf16[1,2,144,512]{3,2,1,0:T(8,128)(2,1)}, f32[512,512]{1,0:T(8,128)S(1)}, f32[512,512]{1,0:T(8,128)S(1)}, f32[16,512]{1,0:T(8,128)S(1)}) custom-call(s32[3]{0:T(128)S(1)} %pad_add_fusion.refs_0_, bf16[2,24,48,512]{3,2,1,0:T(8,128)(2,1)S(1)} %get-tuple-element.40.refs_1_, ...), custom_call_target="tpu_custom_call", output_to_operand_aliasing={{1}: (7, {}), {2}: (8, {}), {3}: (9, {})} | custom-call | flops 50000000 | bytes 1000000 | tf_op jit(solution)/shard_map/pallas_call | solution.py:286
  26.2 1.6 %collective-permute-start.2 = (bf16[1,2,144,512]{3,2,1,0:T(8,128)(2,1)}, bf16[1,2,144,512]{3,2,1,0:T(8,128)(2,1)S(1)}, u32[]{:S(2)}, u32[]{:S(2)}) collective-permute-start(bf16[1,2,144,512]{3,2,1,0:T(8,128)(2,1)} %get-tuple-element.45.refs_2_), channel_id=1, source_target_pairs={{0,2},{1,3},{2,0},{3,1},{4,6},{5,7},{6,4},{7,5},{8,10},{9,11},{10,... | collective-permute-start | bytes 884744 | tf_op jit(solution)/shard_map/ppermute | solution.py:54
  27.8 5.1 %shard_map.105 = (bf16[1,2,144,512]{3,2,1,0:T(8,128)(2,1)}, f32[512,512]{1,0:T(8,128)S(1)}, f32[512,512]{1,0:T(8,128)S(1)}, f32[16,512]{1,0:T(8,128)S(1)}) custom-call(s32[3]{0:T(128)S(1)} %pad_add_fusion.1.refs_0_, bf16[2,24,48,512]{3,2,1,0:T(8,128)(2,1)S(1)} %get-tuple-element.40.refs_1_, ...), custom_call_target="tpu_custom_call", output_to_operand_aliasing={{1}: (8, {}), {2}: (9, {}), {3}: (10, {})} | custom-call | flops 50000000 | bytes 1000000 | tf_op jit(solution)/shard_map/pallas_call | solution.py:286
  32.9 0.4 collective-permute-start.6
  33.4 4.8 %shard_map.106 = (bf16[1,2,144,512]{3,2,1,0:T(8,128)(2,1)}, f32[512,512]{1,0:T(8,128)S(1)}, f32[512,512]{1,0:T(8,128)S(1)}, f32[16,512]{1,0:T(8,128)S(1)}, f32[2...) custom-call(s32[3]{0:T(128)S(1)} %pad_add_fusion.2.refs_0_, ...), custom_call_target="tpu_custom_call", output_to_operand_aliasing={{1}: (10, {}), {2}: (11, {}), {3}: (12, {})} | custom-call | flops 50000000 | bytes 1000000 | tf_op jit(solution)/shard_map/pallas_call | solution.py:286
  38.2 0.5 collective-permute-start.15
  38.7 1.6 %collective-permute-start.7 = (bf16[1,2,144,512]{3,2,1,0:T(8,128)(2,1)}, bf16[1,2,144,512]{3,2,1,0:T(8,128)(2,1)S(1)}, u32[]{:S(2)}, u32[]{:S(2)}) collective-permute-start(bf16[1,2,144,512]{3,2,1,0:T(8,128)(2,1)} %get-tuple-element.56.refs_2_), channel_id=1, source_target_pairs={{0,2},{1,3},{2,0},{3,1},{4,6},{5,7},{6,4},{7,5},{8,10},{9,11},{10,... | collective-permute-start | bytes 884744 | tf_op jit(solution)/shard_map/ppermute | solution.py:54
  40.3 0.5 shard_map.110.refs_4_
  40.8 0.1 collective-permute-start.16
  40.9 1.7 %collective-permute-done.6.refs_3_.refs_6_ = bf16[1,2,144,512]{3,2,1,0:T(8,128)(2,1)S(1)} collective-permute-done((bf16[1,2,144,512]{3,2,1,0:T(8,128)(2,1)}, bf16[1,2,144,512]{3,2,1,0:T(8,128)(2,1)S(1)}, u32[]{:S(2)}, u32[]{:S(2)}) %collective-permute-start.6) | collective-permute-done | bytes 294944 | tf_op jit(solution)/shard_map/ppermute | solution.py:54
  42.7 1.5 %shard_map.111 = bf16[32,72,128]{2,1,0:T(8,128)(2,1)} custom-call(s32[3]{0:T(128)S(1)} %pad_add_fusion.refs_0_, f32[2048,128]{1,0:T(8,128)S(1)} %get-tuple-element.61.refs_1_, bf16[1024,128]{1,0:T(8,128)(2,1)S(1)} %collective-permute-done.14.refs_2_, bf16[1024,128]{1,0:T(8,128)(2,1)S(1)} %collective-permute-done.15.refs_3_, ...), custom_call_target="tpu_custom_call" | custom-call | flops 5000000 | bytes 1000000 | tf_op jit(solution)/shard_map/pallas_call | solution.py:286
  44.2 7.1 %all-to-all-start = ((bf16[32,72,128]{2,1,0:T(8,128)(2,1)}), bf16[32,72,128]{2,1,0:T(8,128)(2,1)S(1)}, u32[]{:S(2)}, u32[]{:S(2)}) async-start(bf16[32,72,128]{2,1,0:T(8,128)(2,1)} %shard_map.111), calls=%async_computation | async-start | bytes 1179648 | tf_op jit(solution)/shard_map/all_to_all | solution.py:560
  51.3 1.7 %shard_map.107 = (bf16[2,2,144,512]{3,2,1,0:T(8,128)(2,1)S(1)}, bf16[2,80,512]{2,1,0:T(8,128)(2,1)S(1)}, bf16[2,96,512]{2,1,0:T(8,128)(2,1)S(1)}, bf16[48,512]{1,0:T(8,128)(2,1)S(1)}) custom-call(s32[3]{0:T(128)S(1)} %pad_add_fusion.refs_0_, bf16[1,2,144,512]{3,2,1,0:T(8,128)(2,1)} %get-tuple-element.50.refs_1_, ...), custom_call_target="tpu_custom_call" | custom-call | flops 8000000000 | bytes 1000000 | tf_op jit(solution)/shard_map/pallas_call | solution.py:286
  53.1 1.5 %collective-permute-start.11 = (bf16[2,96,512]{2,1,0:T(8,128)(2,1)S(1)}, bf16[2,96,512]{2,1,0:T(8,128)(2,1)S(1)}, u32[]{:S(2)}, u32[]{:S(2)}) collective-permute-start(bf16[2,96,512]{2,1,0:T(8,128)(2,1)S(1)} %get-tuple-element.59), channel_id=1, source_target_pairs={{0,4},{4,8},{8,12},{12,16},{16,20},{20,24},{24,28},{28,0},{1,5},{5... | collective-permute-start | bytes 589832 | tf_op jit(solution)/shard_map/ppermute | solution.py:54
  54.6 1.4 %collective-permute-start.10 = (bf16[2,80,512]{2,1,0:T(8,128)(2,1)S(1)}, bf16[2,80,512]{2,1,0:T(8,128)(2,1)S(1)}, u32[]{:S(2)}, u32[]{:S(2)}) collective-permute-start(bf16[2,80,512]{2,1,0:T(8,128)(2,1)S(1)} %get-tuple-element.58), channel_id=1, source_target_pairs={{0,34},{1,35},{2,32},{3,33},{32,66},{33,67},{34,64},{35,65},{64,98... | collective-permute-start | bytes 491528 | tf_op jit(solution)/shard_map/ppermute | solution.py:54
  56.0 3.0 %collective-permute-start.12 = (bf16[48,512]{1,0:T(8,128)(2,1)S(1)}, bf16[48,512]{1,0:T(8,128)(2,1)S(1)}, u32[]{:S(2)}, u32[]{:S(2)}) collective-permute-start(bf16[48,512]{1,0:T(8,128)(2,1)S(1)} %get-tuple-element.60), channel_id=1, source_target_pairs={{0,36},{4,40},{8,44},{12,48},{16,52},{20,56},{24,60},{28,32},{32,6... | collective-permute-start | bytes 147464 | tf_op jit(solution)/shard_map/ppermute | solution.py:54
  58.9 10.5 %all-to-all-done.refs_1_ = bf16[32,72,128]{2,1,0:T(8,128)(2,1)S(1)} async-done(((bf16[32,72,128]{2,1,0:T(8,128)(2,1)}), bf16[32,72,128]{2,1,0:T(8,128)(2,1)S(1)}, u32[]{:S(2)}, u32[]{:S(2)}) %all-to-all-start) | async-done | bytes 589856 | tf_op jit(solution)/shard_map/all_to_all | solution.py:560
  69.5 0.6 shard_map.112.refs_1_
  70.1 3.2 %collective-permute-start.17 = (f32[72,128]{1,0:T(8,128)S(1)}, f32[72,128]{1,0:T(8,128)S(1)}, u32[]{:S(2)}, u32[]{:S(2)}) collective-permute-start(f32[72,128]{1,0:T(8,128)S(1)} %shard_map.112.refs_1_), channel_id=1, source_target_pairs={{0,32},{32,0},{64,96},{96,64},{128,160},{160,128},{192,224},{224,1... | collective-permute-start | bytes 110600 | tf_op jit(solution)/shard_map/ppermute | solution.py:54
  73.3 1.7 %shard_map.104.refs_3_.refs_4_ = bf16[2,2,144,512]{3,2,1,0:T(8,128)(2,1)S(1)} custom-call(s32[3]{0:T(128)S(1)} %pad_add_fusion.refs_0_, bf16[1,2,144,512]{3,2,1,0:T(8,128)(2,1)} %get-tuple-element.39.refs_1_, bf16[1,2,144,512]{3,2,1,0:T(8,128)(2,1)} %get-tuple-element.45.refs_2_, bf16[1,2,144,512]{3,2,1,0:T(8,128)(2,1)S(1)} %collective-permute-done.1.refs_3_.refs_13_, ...), custom_call_target="tpu_custom_call" | custom-call | flops 5000000 | bytes 1000000 | tf_op jit(solution)/shard_map/pallas_call | solution.py:286
  75.0 0.6 shard_map.108.refs_7_.refs_3_
  75.6 0.3 collective-permute-done.17.refs_2_
  75.9 1.4 %shard_map.113 = bf16[32,72,128]{2,1,0:T(8,128)(2,1)} custom-call(s32[3]{0:T(128)S(1)} %pad_add_fusion.refs_0_, f32[72,128]{1,0:T(8,128)S(1)} %shard_map.112.refs_1_, f32[72,128]{1,0:T(8,128)S(1)} %collective-permute-done.17.refs_2_, bf16[400,512]{1,0:T(8,128)(2,1)S(1)} %shard_map.108.refs_7_.refs_3_, bf16[2,2,144,512]{3,2,1,0:T(8,128)(2,1)S(1)} %shard_map.104.refs_3_.refs_4_), custom_call_target="tpu_custom_call" | custom-call | flops 5000000 | bytes 1000000 | tf_op jit(solution)/shard_map/pallas_call | solution.py:286
  77.3 5.2 %all-to-all-start.1 = ((bf16[32,72,128]{2,1,0:T(8,128)(2,1)}), bf16[32,72,128]{2,1,0:T(8,128)(2,1)S(1)}, u32[]{:S(2)}, u32[]{:S(2)}) async-start(bf16[32,72,128]{2,1,0:T(8,128)(2,1)} %shard_map.113), calls=%async_computation.1 | async-start | bytes 1179648 | tf_op jit(solution)/shard_map/all_to_all | solution.py:560
  82.5 0.1 collective-permute-start.8
  82.6 0.5 collective-permute-start.9
  83.1 0.1 collective-permute-start.13
  83.2 1.4 %collective-permute-done.8.refs_5_ = bf16[2,2,144,512]{3,2,1,0:T(8,128)(2,1)S(1)} collective-permute-done((bf16[2,2,144,512]{3,2,1,0:T(8,128)(2,1)S(1)}, bf16[2,2,144,512]{3,2,1,0:T(8,128)(2,1)S(1)}, u32[]{:S(2)}, u32[]{:S(2)}) %collective-permute-start.8) | collective-permute-done | bytes 589856 | tf_op jit(solution)/shard_map/ppermute | solution.py:54
  84.6 0.8 collective-permute-done.9.refs_6_
  85.4 0.6 collective-permute-done.13.refs_8_
  86.0 7.5 %shard_map.109.refs_2_ = bf16[2,24,48,512]{3,2,1,0:T(8,128)(2,1)} custom-call(s32[3]{0:T(128)S(1)} %pad_add_fusion.refs_0_, bf16[2,24,48,512]{3,2,1,0:T(8,128)(2,1)} %refs_1_.5, bf16[2,24,48,512]{3,2,1,0:T(8,128)(2,1)} %refs_2_.5, bf16[2,2,144,512]{3,2,1,0:T(8,128)(2,1)S(1)} %shard_map.104.refs_3_.refs_4_, ...), custom_call_target="tpu_custom_call" | custom-call | flops 5000000 | bytes 1000000 | tf_op jit(solution)/shard_map/pallas_call | solution.py:286
  93.5 6.6 %all-to-all-done.1.refs_1_ = bf16[32,72,128]{2,1,0:T(8,128)(2,1)S(1)} async-done(((bf16[32,72,128]{2,1,0:T(8,128)(2,1)}), bf16[32,72,128]{2,1,0:T(8,128)(2,1)S(1)}, u32[]{:S(2)}, u32[]{:S(2)}) %all-to-all-start.1) | async-done | bytes 589856 | tf_op jit(solution)/shard_map/all_to_all | solution.py:560
  100.2 0.5 shard_map.114.refs_2_
  100.7 0.2 collective-permute-start.18
  100.9 1.6 %shard_map.115 = (f32[3,512,128]{2,1,0:T(8,128)}, f32[128,512]{1,0:T(8,128)}) custom-call(s32[3]{0:T(128)S(1)} %pad_add_fusion.refs_0_, bf16[32,72,128]{2,1,0:T(8,128)(2,1)S(1)} %all-to-all-done.1.refs_1_, f32[8,128]{1,0:T(8,128)S(1)} %shard_map.114.refs_2_), custom_call_target="tpu_custom_call" | custom-call | flops 5000000 | bytes 1000000 | tf_op jit(solution)/shard_map/pallas_call | solution.py:286
  102.5 2.0 %collective-permute-done.18 = f32[8,128]{1,0:T(8,128)S(1)} collective-permute-done((f32[8,128]{1,0:T(8,128)S(1)}, f32[8,128]{1,0:T(8,128)S(1)}, u32[]{:S(2)}, u32[]{:S(2)}) %collective-permute-start.18) | collective-permute-done | bytes 4128 | tf_op jit(solution)/shard_map/ppermute | solution.py:54
  104.4 0.6 slice_bitcast_fusion
  (21 shorter events, 0.2 us)
Async XLA Ops:
  0.8 14.9 %copy-start = (f32[512]{0:T(512)S(1)}, f32[512]{0:T(512)}, u32[]{:S(2)}) copy-start(f32[512]{0:T(512)} %param.8) | copy-start | bytes 6148
  0.8 14.9 %copy-start.1 = (f32[512]{0:T(512)S(1)}, f32[512]{0:T(512)}, u32[]{:S(2)}) copy-start(f32[512]{0:T(512)} %param.9) | copy-start | bytes 6148
  4.2 11.5 %collective-permute-start = (bf16[512,512]{1,0:T(8,128)(2,1)S(1)}, bf16[512,512]{1,0:T(8,128)(2,1)S(1)}, u32[]{:S(2)}, u32[]{:S(2)}) collective-permute-start(bf16[512,512]{1,0:T(8,128)(2,1)S(1)} %get-tuple-element.38.refs_7_.refs_5_.refs_6_.refs_8_), channel_id=1, source_target_pairs={{0,1},{1,0},{2,3},{3,2},{4,5},{5,4},{6,7},{7,6},{8,9},{9,8},{10,11... | collective-permute-start | bytes 1572872 | tf_op jit(solution)/shard_map/ppermute | solution.py:54
  4.3 23.5 %collective-permute-start.3 = (bf16[4,3,32,512]{3,2,1,0:T(8,128)(2,1)}, bf16[4,3,32,512]{3,2,1,0:T(8,128)(2,1)S(1)}, u32[]{:S(2)}, u32[]{:S(2)}) collective-permute-start(bf16[4,3,32,512]{3,2,1,0:T(8,128)(2,1)} %get-tuple-element.46), channel_id=1, source_target_pairs={{0,226},{1,227},{2,224},{3,225},{32,2},{33,3},{34,0},{35,1},{64,34... | collective-permute-start | bytes 1179656 | tf_op jit(solution)/shard_map/ppermute | solution.py:54
  9.6 23.8 %collective-permute-start.4 = (bf16[4,12,8,512]{3,2,1,0:T(8,128)(2,1)}, bf16[4,12,8,512]{3,2,1,0:T(8,128)(2,1)S(1)}, u32[]{:S(2)}, u32[]{:S(2)}) collective-permute-start(bf16[4,12,8,512]{3,2,1,0:T(8,128)(2,1)} %get-tuple-element.51), channel_id=1, source_target_pairs={{0,28},{4,0},{8,4},{12,8},{16,12},{20,16},{24,20},{28,24},{1,29},{... | collective-permute-start | bytes 1179656 | tf_op jit(solution)/shard_map/ppermute | solution.py:54
  9.7 23.7 %collective-permute-start.5 = (bf16[4,3,8,512]{3,2,1,0:T(8,128)(2,1)}, bf16[4,3,8,512]{3,2,1,0:T(8,128)(2,1)S(1)}, u32[]{:S(2)}, u32[]{:S(2)}) collective-permute-start(bf16[4,3,8,512]{3,2,1,0:T(8,128)(2,1)} %get-tuple-element.52), channel_id=1, source_target_pairs={{0,252},{4,224},{8,228},{12,232},{16,236},{20,240},{24,244},{28,24... | collective-permute-start | bytes 294920 | tf_op jit(solution)/shard_map/ppermute | solution.py:54
  20.7 12.8 %collective-permute-start.1 = (bf16[1,2,144,512]{3,2,1,0:T(8,128)(2,1)}, bf16[1,2,144,512]{3,2,1,0:T(8,128)(2,1)S(1)}, u32[]{:S(2)}, u32[]{:S(2)}) collective-permute-start(bf16[1,2,144,512]{3,2,1,0:T(8,128)(2,1)} %get-tuple-element.39.refs_1_), channel_id=1, source_target_pairs={{0,2},{1,3},{2,0},{3,1},{4,6},{5,7},{6,4},{7,5},{8,10},{9,11},{10,... | collective-permute-start | bytes 884744 | tf_op jit(solution)/shard_map/ppermute | solution.py:54
  26.2 14.1 %collective-permute-start.2 = (bf16[1,2,144,512]{3,2,1,0:T(8,128)(2,1)}, bf16[1,2,144,512]{3,2,1,0:T(8,128)(2,1)S(1)}, u32[]{:S(2)}, u32[]{:S(2)}) collective-permute-start(bf16[1,2,144,512]{3,2,1,0:T(8,128)(2,1)} %get-tuple-element.45.refs_2_), channel_id=1, source_target_pairs={{0,2},{1,3},{2,0},{3,1},{4,6},{5,7},{6,4},{7,5},{8,10},{9,11},{10,... | collective-permute-start | bytes 884744 | tf_op jit(solution)/shard_map/ppermute | solution.py:54
  32.9 9.8 %collective-permute-start.6 = (bf16[1,2,144,512]{3,2,1,0:T(8,128)(2,1)}, bf16[1,2,144,512]{3,2,1,0:T(8,128)(2,1)S(1)}, u32[]{:S(2)}, u32[]{:S(2)}) collective-permute-start(bf16[1,2,144,512]{3,2,1,0:T(8,128)(2,1)} %get-tuple-element.50.refs_1_), channel_id=1, source_target_pairs={{0,2},{1,3},{2,0},{3,1},{4,6},{5,7},{6,4},{7,5},{8,10},{9,11},{10,... | collective-permute-start | bytes 884744 | tf_op jit(solution)/shard_map/ppermute | solution.py:54
  38.2 4.5 %collective-permute-start.14 = (bf16[1024,128]{1,0:T(8,128)(2,1)S(1)}, bf16[1024,128]{1,0:T(8,128)(2,1)S(1)}, u32[]{:S(2)}, u32[]{:S(2)}) collective-permute-start(bf16[1024,128]{1,0:T(8,128)(2,1)S(1)} %get-tuple-element.62), channel_id=1, source_target_pairs={{0,1},{1,0},{2,3},{3,2},{4,5},{5,4},{6,7},{7,6},{8,9},{9,8},{10,11... | collective-permute-start | bytes 786440 | tf_op jit(solution)/shard_map/ppermute | solution.py:54
  38.2 4.5 %collective-permute-start.15 = (bf16[1024,128]{1,0:T(8,128)(2,1)S(1)}, bf16[1024,128]{1,0:T(8,128)(2,1)S(1)}, u32[]{:S(2)}, u32[]{:S(2)}) collective-permute-start(bf16[1024,128]{1,0:T(8,128)(2,1)S(1)} %get-tuple-element.63), channel_id=1, source_target_pairs={{0,1},{1,0},{2,3},{3,2},{4,5},{5,4},{6,7},{7,6},{8,9},{9,8},{10,11... | collective-permute-start | bytes 786440 | tf_op jit(solution)/shard_map/ppermute | solution.py:54
  38.7 12.6 %collective-permute-start.7 = (bf16[1,2,144,512]{3,2,1,0:T(8,128)(2,1)}, bf16[1,2,144,512]{3,2,1,0:T(8,128)(2,1)S(1)}, u32[]{:S(2)}, u32[]{:S(2)}) collective-permute-start(bf16[1,2,144,512]{3,2,1,0:T(8,128)(2,1)} %get-tuple-element.56.refs_2_), channel_id=1, source_target_pairs={{0,2},{1,3},{2,0},{3,1},{4,6},{5,7},{6,4},{7,5},{8,10},{9,11},{10,... | collective-permute-start | bytes 884744 | tf_op jit(solution)/shard_map/ppermute | solution.py:54
  40.8 1.8 %collective-permute-start.16 = (f32[8,128]{1,0:T(8,128)S(1)}, f32[8,128]{1,0:T(8,128)S(1)}, u32[]{:S(2)}, u32[]{:S(2)}) collective-permute-start(f32[8,128]{1,0:T(8,128)S(1)} %shard_map.110.refs_4_), channel_id=1, source_target_pairs={{0,1},{1,0},{2,3},{3,2},{4,5},{5,4},{6,7},{7,6},{8,9},{9,8},{10,11... | collective-permute-start | bytes 12296 | tf_op jit(solution)/shard_map/ppermute | solution.py:54
  44.2 25.3 %all-to-all-start = ((bf16[32,72,128]{2,1,0:T(8,128)(2,1)}), bf16[32,72,128]{2,1,0:T(8,128)(2,1)S(1)}, u32[]{:S(2)}, u32[]{:S(2)}) async-start(bf16[32,72,128]{2,1,0:T(8,128)(2,1)} %shard_map.111), calls=%async_computation | async-start | bytes 1179648 | tf_op jit(solution)/shard_map/all_to_all | solution.py:560
  53.1 21.9 %collective-permute-start.11 = (bf16[2,96,512]{2,1,0:T(8,128)(2,1)S(1)}, bf16[2,96,512]{2,1,0:T(8,128)(2,1)S(1)}, u32[]{:S(2)}, u32[]{:S(2)}) collective-permute-start(bf16[2,96,512]{2,1,0:T(8,128)(2,1)S(1)} %get-tuple-element.59), channel_id=1, source_target_pairs={{0,4},{4,8},{8,12},{12,16},{16,20},{20,24},{24,28},{28,0},{1,5},{5... | collective-permute-start | bytes 589832 | tf_op jit(solution)/shard_map/ppermute | solution.py:54
  54.6 20.4 %collective-permute-start.10 = (bf16[2,80,512]{2,1,0:T(8,128)(2,1)S(1)}, bf16[2,80,512]{2,1,0:T(8,128)(2,1)S(1)}, u32[]{:S(2)}, u32[]{:S(2)}) collective-permute-start(bf16[2,80,512]{2,1,0:T(8,128)(2,1)S(1)} %get-tuple-element.58), channel_id=1, source_target_pairs={{0,34},{1,35},{2,32},{3,33},{32,66},{33,67},{34,64},{35,65},{64,98... | collective-permute-start | bytes 491528 | tf_op jit(solution)/shard_map/ppermute | solution.py:54
  56.0 19.0 %collective-permute-start.12 = (bf16[48,512]{1,0:T(8,128)(2,1)S(1)}, bf16[48,512]{1,0:T(8,128)(2,1)S(1)}, u32[]{:S(2)}, u32[]{:S(2)}) collective-permute-start(bf16[48,512]{1,0:T(8,128)(2,1)S(1)} %get-tuple-element.60), channel_id=1, source_target_pairs={{0,36},{4,40},{8,44},{12,48},{16,52},{20,56},{24,60},{28,32},{32,6... | collective-permute-start | bytes 147464 | tf_op jit(solution)/shard_map/ppermute | solution.py:54
  70.1 5.8 %collective-permute-start.17 = (f32[72,128]{1,0:T(8,128)S(1)}, f32[72,128]{1,0:T(8,128)S(1)}, u32[]{:S(2)}, u32[]{:S(2)}) collective-permute-start(f32[72,128]{1,0:T(8,128)S(1)} %shard_map.112.refs_1_), channel_id=1, source_target_pairs={{0,32},{32,0},{64,96},{96,64},{128,160},{160,128},{192,224},{224,1... | collective-permute-start | bytes 110600 | tf_op jit(solution)/shard_map/ppermute | solution.py:54
  77.3 22.9 %all-to-all-start.1 = ((bf16[32,72,128]{2,1,0:T(8,128)(2,1)}), bf16[32,72,128]{2,1,0:T(8,128)(2,1)S(1)}, u32[]{:S(2)}, u32[]{:S(2)}) async-start(bf16[32,72,128]{2,1,0:T(8,128)(2,1)} %shard_map.113), calls=%async_computation.1 | async-start | bytes 1179648 | tf_op jit(solution)/shard_map/all_to_all | solution.py:560
  82.5 2.1 %collective-permute-start.8 = (bf16[2,2,144,512]{3,2,1,0:T(8,128)(2,1)S(1)}, bf16[2,2,144,512]{3,2,1,0:T(8,128)(2,1)S(1)}, u32[]{:S(2)}, u32[]{:S(2)}) collective-permute-start(bf16[2,2,144,512]{3,2,1,0:T(8,128)(2,1)S(1)} %shard_map.104.refs_3_.refs_4_), channel_id=1, source_target_pairs={{0,1},{1,0},{2,3},{3,2},{4,5},{5,4},{6,7},{7,6},{8,9},{9,8},{10,11... | collective-permute-start | bytes 1769480 | tf_op jit(solution)/shard_map/ppermute | solution.py:54
  82.6 2.8 %collective-permute-start.9 = (bf16[2,2,144,512]{3,2,1,0:T(8,128)(2,1)S(1)}, bf16[2,2,144,512]{3,2,1,0:T(8,128)(2,1)S(1)}, u32[]{:S(2)}, u32[]{:S(2)}) collective-permute-start(bf16[2,2,144,512]{3,2,1,0:T(8,128)(2,1)S(1)} %get-tuple-element.57.refs_4_), channel_id=1, source_target_pairs={{0,1},{1,0},{2,3},{3,2},{4,5},{5,4},{6,7},{7,6},{8,9},{9,8},{10,11... | collective-permute-start | bytes 1769480 | tf_op jit(solution)/shard_map/ppermute | solution.py:54
  83.1 2.9 %collective-permute-start.13 = (bf16[400,512]{1,0:T(8,128)(2,1)S(1)}, bf16[400,512]{1,0:T(8,128)(2,1)S(1)}, u32[]{:S(2)}, u32[]{:S(2)}) collective-permute-start(bf16[400,512]{1,0:T(8,128)(2,1)S(1)} %shard_map.108.refs_7_.refs_3_), channel_id=1, source_target_pairs={{0,1},{1,0},{2,3},{3,2},{4,5},{5,4},{6,7},{7,6},{8,9},{9,8},{10,11... | collective-permute-start | bytes 1228808 | tf_op jit(solution)/shard_map/ppermute | solution.py:54
  100.7 3.7 %collective-permute-start.18 = (f32[8,128]{1,0:T(8,128)S(1)}, f32[8,128]{1,0:T(8,128)S(1)}, u32[]{:S(2)}, u32[]{:S(2)}) collective-permute-start(f32[8,128]{1,0:T(8,128)S(1)} %shard_map.114.refs_2_), channel_id=1, source_target_pairs={{0,2},{1,3},{2,0},{3,1},{4,6},{5,7},{6,4},{7,5},{8,10},{9,11},{10,... | collective-permute-start | bytes 12296 | tf_op jit(solution)/shard_map/ppermute | solution.py:54
